TPU v7x, 32 devices: a whole 2x2x4 slice. The times are simulated.
32 devices in a mesh: sy: 4 (over z), sx: 4 (over y, core), tp: 2 (over x).
Axes of the slice: x: 2, y: 2, z: 4, core: 2. Of those that a mesh axis runs over, the one named last changes fastest.
Arguments:
- features: bfloat16 [96, 64, 1408], P('sy', 'sx', 'tp'), may hold values from -6 to 6
- depth_kernel: float32 [7, 7, 1408], P(None, None, 'tp'), may hold values from -0.875 to 0.875
- depth_bias: float32 [1408], P('tp'), may hold values from -1 to 1
- norm_gain: float32 [1408], replicated, may hold values from 0.1 to 1.9
- norm_bias: float32 [1408], replicated, may hold values from -3 to 3
- up_weight: bfloat16 [1408, 5632], P(None, 'tp'), may hold values from -0.15625 to 0.15625
- up_bias: float32 [5632], P('tp'), may hold values from -3 to 3
- response_gain: float32 [5632], P('tp'), may hold values from -4 to 4
- response_shift: float32 [5632], P('tp'), may hold values from -3 to 3
- down_weight: bfloat16 [5632, 1408], P('tp', ('sy', 'sx')), may hold values from -0.078125 to 0.078125
- down_bias: float32 [1408], P('tp'), may hold values from -3 to 3
- tissue: int32 [12, 8], P('sy', 'sx'), may hold values from 0 to 1, as said below
- cotangent: bfloat16 [96, 64, 1408], P('sy', 'sx', 'tp'), may hold values from -6 to 6
Outputs:
- block_out: bfloat16 [96, 64, 1408], P('sy', 'sx', 'tp')
- feature_grad: bfloat16 [96, 64, 1408], P('sy', 'sx', 'tp')
Inputs may be any that keep to these rules, and one draw needn't show every extreme that they name: Each device's block of 3 x 2 tiles holds 1 to 4 tissue tiles; some device's block holds exactly 4.
All inputs are finite; a program needn't handle non-finite values.
Results may differ from a plain program's by a relative error of at most 0.0049.
The roundings to bfloat16 on the way count: a program that leaves them out, or rounds other values in their place, can miss the bound.
Values may be sent and summed in bfloat16 or wider, within the bound.
A program may use at most 128 MiB of HBM per device.

v0:
```python
import jax
import jax.numpy as jnp
from jax import lax
from jax.sharding import PartitionSpec as P

KERNEL = 7
TILE = 8
root_half = 0.7071067811865476
root_two_pi_inv = 0.3989422804014327


def extended(block, sides, width):
    for axis, dim in sides:
        count = lax.axis_size(axis)
        forward = [(i, i + 1) for i in range(count - 1)]
        backward = [(target, source) for source, target in forward]
        low = lax.ppermute(
            lax.slice_in_dim(block, block.shape[dim] - width, None, axis=dim), axis, forward
        )
        high = lax.ppermute(lax.slice_in_dim(block, 0, width, axis=dim), axis, backward)
        block = jnp.concatenate([low, block, high], axis=dim)
    return block


def gelu_value(values):
    return 0.5 * values * (1.0 + jax.scipy.special.erf(values * root_half))


def gelu_slope(values):
    return (
        0.5 * (1.0 + jax.scipy.special.erf(values * root_half))
        + values * jnp.exp(-0.5 * values * values) * root_two_pi_inv
    )


def depthwise(padded, kernel, rows_out, cols_out, flipped):
    summed = jnp.zeros((rows_out, cols_out, kernel.shape[2]), jnp.float32)
    last_tap = KERNEL - 1
    for row_tap in range(KERNEL):
        for col_tap in range(KERNEL):
            row_start = last_tap - row_tap if flipped else row_tap
            col_start = last_tap - col_tap if flipped else col_tap
            window = padded[row_start : row_start + rows_out, col_start : col_start + cols_out]
            summed = summed + window.astype(jnp.float32) * kernel[row_tap, col_tap]
    return summed


def extend(image):
    return extended(image, (("sy", 0), ("sx", 1)), KERNEL // 2)


def all_channels(rows_array):
    return lax.all_gather(rows_array, "tp", axis=1, tiled=True)


def global_vector(local_part):
    hidden_local = local_part.shape[0]
    placed = lax.dynamic_update_slice(
        jnp.zeros((hidden_local * lax.axis_size("tp"),), jnp.float32),
        local_part,
        (lax.axis_index("tp") * hidden_local,),
    )
    return lax.psum(placed, ("sy", "sx", "tp"))


def shards(
    features,
    depth_kernel,
    depth_bias,
    norm_gain,
    norm_bias,
    up_weight,
    up_bias,
    response_gain,
    response_shift,
    down_weight,
    down_bias,
    tissue,
    cotangent,
):
    image_rows, image_cols, local_channels = features.shape
    hidden_local = up_weight.shape[1]
    channel_start = lax.axis_index("tp") * local_channels
    contract_last = (((1,), (1,)), ((), ()))
    pixel_mask = jnp.repeat(jnp.repeat(tissue, TILE, axis=0), TILE, axis=1).astype(jnp.float32)
    mask_rows = pixel_mask.reshape(-1)

    def select(image):
        return image.reshape(image_rows * image_cols, image.shape[2])

    def restore(rows_array):
        return rows_array.reshape(image_rows, image_cols, rows_array.shape[1])

    convolved = (
        depthwise(extend(features), depth_kernel, image_rows, image_cols, False) + depth_bias
    ).astype(jnp.bfloat16)
    gathered = all_channels(select(convolved)).astype(jnp.float32)
    centre = jnp.mean(gathered, axis=1, keepdims=True)
    spread = jnp.mean(jnp.square(gathered - centre), axis=1, keepdims=True)
    inv_scale = lax.rsqrt(spread + 1e-06)
    standard = (gathered - centre) * inv_scale
    normed = (standard * norm_gain + norm_bias).astype(jnp.bfloat16)
    preact = jnp.dot(normed, up_weight, preferred_element_type=jnp.float32) + up_bias
    hidden = gelu_value(preact).astype(jnp.bfloat16)
    hidden_wide = hidden.astype(jnp.float32)
    squares = global_vector(jnp.sum(mask_rows[:, None] * hidden_wide * hidden_wide, axis=0))
    all_norms = jnp.sqrt(squares)
    norm_level = jnp.mean(all_norms) + 1e-06
    unit_start = lax.axis_index("tp") * hidden_local
    column_norms = lax.dynamic_slice_in_dim(all_norms, unit_start, hidden_local)
    norm_ratio = column_norms / norm_level
    response = (response_gain * hidden_wide * norm_ratio + response_shift + hidden_wide).astype(
        jnp.bfloat16
    )
    down_whole = lax.all_gather(down_weight, ("sy", "sx"), axis=1, tiled=True)
    partial_out = jnp.dot(response, down_whole, preferred_element_type=jnp.float32)
    branch = lax.psum_scatter(partial_out, "tp", scatter_dimension=1, tiled=True)
    branch_image = restore(branch + down_bias)
    block_out = (features.astype(jnp.float32) + pixel_mask[:, :, None] * branch_image).astype(
        jnp.bfloat16
    )
    masked_cot = (select(cotangent).astype(jnp.float32) * mask_rows[:, None]).astype(jnp.bfloat16)
    cot_wide = all_channels(masked_cot)
    back_hidden = lax.dot_general(
        cot_wide, down_whole, contract_last, preferred_element_type=jnp.float32
    )
    ratio_grad = global_vector(response_gain * jnp.sum(back_hidden * hidden_wide, axis=0))
    ratio_local = lax.dynamic_slice_in_dim(ratio_grad, unit_start, hidden_local)
    norms_grad = ratio_local / norm_level - jnp.sum(ratio_grad * all_norms) / (
        all_norms.shape[0] * norm_level * norm_level
    )
    hidden_grad = (
        back_hidden * (response_gain * norm_ratio + 1.0)
        + norms_grad * mask_rows[:, None] * hidden_wide / column_norms
    )
    preact_grad = (hidden_grad * gelu_slope(preact)).astype(jnp.bfloat16)
    grad_terms = lax.dot_general(
        preact_grad, up_weight, contract_last, preferred_element_type=jnp.float32
    )
    normed_grad = lax.psum(grad_terms, "tp")
    scaled = normed_grad * norm_gain
    convolved_grad = inv_scale * (
        scaled
        - jnp.mean(scaled, axis=1, keepdims=True)
        - standard * jnp.mean(scaled * standard, axis=1, keepdims=True)
    )
    convolved_grad = convolved_grad.astype(jnp.bfloat16)
    local_grad = lax.dynamic_slice_in_dim(convolved_grad, channel_start, local_channels, 1)
    grad_image = restore(local_grad)
    feature_grad = (
        cotangent.astype(jnp.float32)
        + depthwise(extend(grad_image), depth_kernel, image_rows, image_cols, True)
    ).astype(jnp.bfloat16)
    return (block_out, feature_grad)


def solution(mesh):
    placed = (
        P("sy", "sx", "tp"),
        P(None, None, "tp"),
        P("tp"),
        P(),
        P(),
        P(None, "tp"),
        P("tp"),
        P("tp"),
        P("tp"),
        P("tp", ("sy", "sx")),
        P("tp"),
        P("sy", "sx"),
        P("sy", "sx", "tp"),
    )
    return jax.shard_map(
        shards,
        mesh=mesh,
        in_specs=placed,
        out_specs=(P("sy", "sx", "tp"), P("sy", "sx", "tp")),
        check_vma=False,
    )
```

profile of v0, /device:TPU:0, one launch (start us, length us, event | category | flops | bytes accessed | tf_op | source)
XLA Modules:
  0.0 338.2 jit_solution(16324802515780690744)
XLA Ops:
  7.2 0.0 all-gather.4.cloned.1.call-start
  7.2 0.9 fusion.105
  8.1 4.9 %collective-permute-start = (bf16[3,16,704]{2,1,0:T(8,128)(2,1)S(1)}, bf16[3,16,704]{2,1,0:T(8,128)(2,1)S(1)}, u32[]{:S(2)}, u32[]{:S(2)}) collective-permute-start(bf16[3,16,704]{2,1,0:T(8,128)(2,1)S(1)} %get-tuple-element.77), channel_id=1, source_target_pairs={{0,8},{8,16},{16,24},{1,9},{9,17},{17,25},{2,10},{10,18},{18,26},{... | collective-permute-start | bytes 202760 | tf_op jit(solution)/shard_map/ppermute | solution.py:17
  13.1 1.3 collective-permute-start.1
  14.4 1.4 slice_reduce_fusion.48
  15.8 1.1 slice_reduce_fusion.46
  16.9 1.2 constant_dynamic-update-slice_fusion.3
  18.2 1.2 collective-permute-done.1
  19.3 0.1 fusion.103
  19.5 1.3 collective-permute-start.2
  20.8 1.3 collective-permute-start.3
  22.1 1.4 slice_reduce_fusion.47
  23.5 2.4 collective-permute-done.3
  25.9 14.1 %add_convert_fusion.2 = bf16[24,16,704]{2,1,0:T(8,128)(2,1)S(1)} fusion(bf16[24,16,704]{2,1,0:T(8,128)(2,1)S(1)} %copy-done, bf16[30,16,704]{2,1,0:T(8,128)(2,1)S(1)} %get-tuple-element.81, bf16[30,3,704]{2,1,0:T(4,128)(2,1)S(1)} %collective-permute-done.3, bf16[30,3,704]{2,1,0:T(4,128)(2,1)S(1)} %collective-permute-done.2, ...), kind=kLoop, calls=%fused_computation.149 | loop fusion | flops 74072064 | bytes 5395456 | tf_op jit(solution)/shard_map/convert_element_type | solution.py:96
  40.0 1.0 copy.21
  41.0 0.0 all-gather.4.cloned.1.call-update
  41.0 0.0 all-gather.8.cloned.1.call-start
  41.1 0.1 broadcast_in_dim.4
  41.2 0.1 convert_element_type.364
  41.3 0.1 copy.26
  41.4 0.1 broadcast_in_dim.5.clone
  41.4 0.1 convert_element_type.419
  41.6 0.2 copy.25
  41.8 0.9 multiply_convert_fusion.1
  42.7 0.0 all-gather.8.cloned.1.call-update
  42.7 0.0 all-gather.6.cloned.1.call-start
  42.7 0.7 all-gather.6.cloned.1.call-update
  43.4 0.0 all-reduce.3.cloned.1.call-start
  43.5 23.3 %all-gather.4.cloned.1.call-done = bf16[384,1408]{0,1:T(8,128)(2,1)} async-done(((bf16[384,704]{0,1:T(8,128)(2,1)}), bf16[384,1408]{0,1:T(8,128)(2,1)}) %all-gather.4.cloned.1.call-update) | async-done | bytes 1081360 | tf_op jit(solution)/shard_map/all_gather | solution.py:53
  66.7 1.7 copy.22
  68.5 0.2 convert_reduce_fusion
  68.7 0.4 fusion.15
  69.2 0.0 copy-done.7
  69.2 8.6 %convolution_add_fusion = f32[384,2816]{1,0:T(8,128)} fusion(bf16[1408,2816]{1,0:T(8,128)(2,1)} %param.18, f32[2816]{0:T(1024)S(1)} %copy-done.7, f32[1408]{0:T(1024)S(1)} %copy-done.9, f32[1408]{0:T(1024)S(1)} %copy-done.3, bf16[384,1408]{1,0:T(8,128)(2,1)S(1)} %copy.22, f32[384]{0:T(512)S(1)} %add_rsqrt_fusion, f32[384]{0:T(512)S(1)} %broadcast_multiply_fusion.3), kind=kOutput, calls=%fused_computation.62 | convolution fusion | flops 3049390080 | bytes 13362176 | tf_op jit(solution)/shard_map/dot_general | solution.py:103
  77.8 12.8 %all-gather.8.cloned.1.call-done = bf16[384,1408]{0,1:T(8,128)(2,1)} async-done(((bf16[384,704]{0,1:T(8,128)(2,1)}), bf16[384,1408]{0,1:T(8,128)(2,1)}) %all-gather.8.cloned.1.call-update) | async-done | bytes 1081360 | tf_op jit(solution)/shard_map/all_gather | solution.py:53
  90.6 74.2 %all-gather.6.cloned.1.call-done = bf16[2816,1408]{0,1:T(8,128)(2,1)} async-done(((bf16[2816,88]{0,1:T(8,128)(2,1)}), bf16[2816,1408]{0,1:T(8,128)(2,1)}) %all-gather.6.cloned.1.call-update) | async-done | bytes 7929872 | tf_op jit(solution)/shard_map/all_gather | solution.py:115
  164.8 9.9 %fusion.10 = (f32[2816]{0:T(1024)S(1)}, f32[2816]{0:T(1024)S(1)}, bf16[384,2816]{1,0:T(8,128)(2,1)}, f32[384,2816]{1,0:T(8,128)}) fusion(f32[384]{0:T(512)S(1)} %convert_element_type.419, f32[384,2816]{1,0:T(8,128)} %convolution_add_fusion, bf16[384,1408]{0,1:T(8,128)(2,1)} %all-gather.8.cloned.1.call-done, bf16[2816,1408]{0,1:T(8,128)(2,1)} %all-gather.6.cloned.1.call-done), kind=kOutput, calls=%fused_computation.57 | convolution fusion | flops 3056953856 | bytes 19848704 | tf_op jit(solution)/shard_map/dot_general | solution.py:124
  174.7 0.3 dynamic_update_slice.6
  175.0 0.1 multiply_dynamic-update-slice_fusion
  175.2 39.6 %all-reduce = (f32[5632]{0:T(1024)S(1)}, f32[5632]{0:T(1024)S(1)}) all-reduce(f32[5632]{0:T(1024)S(1)} %dynamic_update_slice.6, f32[5632]{0:T(1024)S(1)} %multiply_dynamic-update-slice_fusion), channel_id=1, replica_groups=mesh['sy'=4,'sx'=4,'tp'=2] {'sy','sx','tp'}, use_global_device_ids=true, to_apply=%region_3.0 | all-reduce | flops 11264 | bytes 90112 | tf_op jit(solution)/shard_map/psum | solution.py:63
  214.7 0.6 multiply_reduce_fusion.1
  216.6 0.1 multiply_add_fusion
  216.7 12.4 %fusion.21 = f32[384,1408]{1,0:T(8,128)} fusion(bf16[1408,2816]{1,0:T(8,128)(2,1)} %param.18, f32[384,2816]{1,0:T(8,128)} %convolution_add_fusion, bf16[384,2816]{1,0:T(8,128)(2,1)} %get-tuple-element.63, f32[384,2816]{1,0:T(8,128)} %get-tuple-element.83, f32[2816]{0:T(1024)S(1)} %get-tuple-element.62, f32[2816]{0:T(1024)S(1)} %get-tuple-element.84, ...), kind=kOutput, calls=%fused_computation.74 | convolution fusion | flops 3062366208 | bytes 20941312 | tf_op jit(solution)/shard_map/dot_general | solution.py:137
  229.1 0.0 reduce-scatter.2.cloned.1.call-start
  229.2 0.6 copy-done.8
  229.8 9.6 %fusion.16 = f32[384,1408]{0,1:T(8,128)} fusion(bf16[2816,1408]{0,1:T(8,128)(2,1)} %all-gather.6.cloned.1.call-done, bf16[384,2816]{1,0:T(8,128)(2,1)} %get-tuple-element.63, f32[2816]{0:T(1024)S(1)} %copy-done.8, f32[2816]{0:T(1024)S(1)} %get-tuple-element.61, f32[2816]{0:T(1024)S(1)} %copy-done.2), kind=kOutput, calls=%fused_computation.68 | convolution fusion | flops 3051552768 | bytes 12289024 | tf_op jit(solution)/shard_map/dot_general | solution.py:116
  239.4 54.7 %all-reduce.3.cloned.1.call-done = f32[384,1408]{1,0:T(8,128)} async-done(((f32[384,1408]{1,0:T(8,128)}), f32[384,1408]{1,0:T(8,128)}) %all-reduce.3.cloned.1.call-update) | async-done | bytes 2162704 | tf_op jit(solution)/shard_map/psum | solution.py:140
  294.1 2.3 fusion.102
  296.4 1.0 fusion.51
  297.4 3.4 %collective-permute-start.4 = (bf16[3,16,704]{2,1,0:T(8,128)(2,1)S(1)}, bf16[3,16,704]{2,1,0:T(8,128)(2,1)S(1)}, u32[]{:S(2)}, u32[]{:S(2)}) collective-permute-start(bf16[3,16,704]{2,1,0:T(8,128)(2,1)S(1)} %bitcast.23), channel_id=1, source_target_pairs={{0,8},{8,16},{16,24},{1,9},{9,17},{17,25},{2,10},{10,18},{18,26},{... | collective-permute-start | bytes 202760 | tf_op jit(solution)/shard_map/ppermute | solution.py:17
  300.8 1.3 collective-permute-start.5
  302.1 0.7 collective-permute-done.4
  302.7 4.3 %collective-permute-done.5 = bf16[3,16,704]{2,1,0:T(8,128)(2,1)S(1)} collective-permute-done((bf16[3,16,704]{2,1,0:T(8,128)(2,1)S(1)}, bf16[3,16,704]{2,1,0:T(8,128)(2,1)S(1)}, u32[]{:S(2)}, u32[]{:S(2)}) %collective-permute-start.5) | collective-permute-done | bytes 67616 | tf_op jit(solution)/shard_map/ppermute | solution.py:20
  307.0 0.2 pad_maximum_fusion.7
  307.2 1.3 collective-permute-start.6
  308.5 3.3 collective-permute-start.7
  311.8 0.1 copy.20
  311.8 0.7 collective-permute-done.7
  312.6 0.6 pad_maximum_fusion
  313.1 10.3 %add_convert_fusion.1 = bf16[24,16,704]{2,1,0:T(8,128)(2,1)} fusion(bf16[24,16,704]{2,1,0:T(8,128)(2,1)S(1)} %bitcast.18, bf16[3,16,704]{2,1,0:T(8,128)(2,1)S(1)} %collective-permute-done.4, bf16[3,16,704]{2,1,0:T(8,128)(2,1)S(1)} %collective-permute-done.5, bf16[30,19,704]{2,1,0:T(8,128)(2,1)S(1)} %get-tuple-element.66, ...), kind=kLoop, calls=%fused_computation.148 | loop fusion | flops 41902080 | bytes 24603392 | tf_op jit(solution)/shard_map/convert_element_type | solution.py:153
  323.5 5.4 %reduce-scatter.2.cloned.1.call-done = f32[384,704]{0,1:T(8,128)} async-done(((f32[384,1408]{0,1:T(8,128)}), f32[384,704]{0,1:T(8,128)}) %reduce-scatter.2.cloned.1.call-update) | async-done | bytes 1081360 | tf_op jit(solution)/shard_map/reduce_scatter | solution.py:117
  328.9 1.4 broadcast_add_fusion
  330.3 0.4 copy.24
  330.7 1.0 fusion.48
  (34 shorter events, 0.2 us)
Async XLA Ops:
  7.2 59.6 %all-gather.4.cloned.1.call-start = ((), (), s32[]{:S(2)}) async-start(), calls=%async_computation.1 | async-start | bytes 1622016 | tf_op jit(solution)/shard_map/all_gather | solution.py:53
  8.1 8.8 %collective-permute-start = (bf16[3,16,704]{2,1,0:T(8,128)(2,1)S(1)}, bf16[3,16,704]{2,1,0:T(8,128)(2,1)S(1)}, u32[]{:S(2)}, u32[]{:S(2)}) collective-permute-start(bf16[3,16,704]{2,1,0:T(8,128)(2,1)S(1)} %get-tuple-element.77), channel_id=1, source_target_pairs={{0,8},{8,16},{16,24},{1,9},{9,17},{17,25},{2,10},{10,18},{18,26},{... | collective-permute-start | bytes 202760 | tf_op jit(solution)/shard_map/ppermute | solution.py:17
  13.1 6.2 %collective-permute-start.1 = (bf16[3,16,704]{2,1,0:T(8,128)(2,1)S(1)}, bf16[3,16,704]{2,1,0:T(8,128)(2,1)S(1)}, u32[]{:S(2)}, u32[]{:S(2)}) collective-permute-start(bf16[3,16,704]{2,1,0:T(8,128)(2,1)S(1)} %get-tuple-element.76), channel_id=1, source_target_pairs={{8,0},{16,8},{24,16},{9,1},{17,9},{25,17},{10,2},{18,10},{26,18},{... | collective-permute-start | bytes 202760 | tf_op jit(solution)/shard_map/ppermute | solution.py:20
  18.1 7.7 %copy-start = (bf16[24,16,704]{2,1,0:T(8,128)(2,1)S(1)}, bf16[24,16,704]{2,1,0:T(8,128)(2,1)}, u32[]{:S(2)}) copy-start(bf16[24,16,704]{2,1,0:T(8,128)(2,1)} %param.13) | copy-start | bytes 1622020
  18.1 7.7 %copy-start.5 = (f32[704]{0:T(1024)S(1)}, f32[704]{0:T(1024)}, u32[]{:S(2)}) copy-start(f32[704]{0:T(1024)} %param.15) | copy-start | bytes 8452
  19.5 4.0 %collective-permute-start.2 = (bf16[30,3,704]{2,1,0:T(4,128)(2,1)S(1)}, bf16[30,3,704]{2,1,0:T(4,128)(2,1)S(1)}, u32[]{:S(2)}, u32[]{:S(2)}) collective-permute-start(bf16[30,3,704]{2,1,0:T(4,128)(2,1)S(1)} %get-tuple-element.69), channel_id=1, source_target_pairs={{0,2},{2,4},{4,6},{1,3},{3,5},{5,7},{8,10},{10,12},{12,14},{9,11},... | collective-permute-start | bytes 380168 | tf_op jit(solution)/shard_map/ppermute | solution.py:17
  20.8 5.1 %collective-permute-start.3 = (bf16[30,3,704]{2,1,0:T(4,128)(2,1)S(1)}, bf16[30,3,704]{2,1,0:T(4,128)(2,1)S(1)}, u32[]{:S(2)}, u32[]{:S(2)}) collective-permute-start(bf16[30,3,704]{2,1,0:T(4,128)(2,1)S(1)} %get-tuple-element.70), channel_id=1, source_target_pairs={{2,0},{4,2},{6,4},{3,1},{5,3},{7,5},{10,8},{12,10},{14,12},{11,9},... | collective-permute-start | bytes 380168 | tf_op jit(solution)/shard_map/ppermute | solution.py:20
  40.0 1.1 copy-start.6
  40.0 1.6 copy-start.1
  41.0 49.5 %all-gather.8.cloned.1.call-start = ((), (), s32[]{:S(2)}) async-start(), calls=%async_computation.4 | async-start | bytes 1622016 | tf_op jit(solution)/shard_map/all_gather | solution.py:53
  42.7 122.1 %all-gather.6.cloned.1.call-start = ((), (), s32[]{:S(2)}) async-start(), calls=%async_computation.2 | async-start | bytes 8425472 | tf_op jit(solution)/shard_map/all_gather | solution.py:115
  43.4 250.7 %all-reduce.3.cloned.1.call-start = ((), (), s32[]{:S(2)}) async-start(), calls=%async_computation.5 | async-start | bytes 4325376 | tf_op jit(solution)/shard_map/psum | solution.py:140
  68.5 0.7 copy-start.3
  68.5 0.7 copy-start.7
  68.5 0.7 copy-start.9
  77.8 97.2 %copy-start.2 = (f32[2816]{0:T(1024)S(1)}, f32[2816]{0:T(1024)}, u32[]{:S(2)}) copy-start(f32[2816]{0:T(1024)} %param.20) | copy-start | bytes 33796
  229.1 0.7 copy-start.8
  229.1 99.8 %reduce-scatter.2.cloned.1.call-start = ((), (), s32[]{:S(2)}) async-start(), calls=%async_computation.3 | async-start | bytes 3244032 | tf_op jit(solution)/shard_map/reduce_scatter | solution.py:117
  297.4 5.4 %collective-permute-start.4 = (bf16[3,16,704]{2,1,0:T(8,128)(2,1)S(1)}, bf16[3,16,704]{2,1,0:T(8,128)(2,1)S(1)}, u32[]{:S(2)}, u32[]{:S(2)}) collective-permute-start(bf16[3,16,704]{2,1,0:T(8,128)(2,1)S(1)} %bitcast.23), channel_id=1, source_target_pairs={{0,8},{8,16},{16,24},{1,9},{9,17},{17,25},{2,10},{10,18},{18,26},{... | collective-permute-start | bytes 202760 | tf_op jit(solution)/shard_map/ppermute | solution.py:17
  300.8 6.2 %collective-permute-start.5 = (bf16[3,16,704]{2,1,0:T(8,128)(2,1)S(1)}, bf16[3,16,704]{2,1,0:T(8,128)(2,1)S(1)}, u32[]{:S(2)}, u32[]{:S(2)}) collective-permute-start(bf16[3,16,704]{2,1,0:T(8,128)(2,1)S(1)} %bitcast.22), channel_id=1, source_target_pairs={{8,0},{16,8},{24,16},{9,1},{17,9},{25,17},{10,2},{18,10},{26,18},{... | collective-permute-start | bytes 202760 | tf_op jit(solution)/shard_map/ppermute | solution.py:20
  307.2 4.7 %collective-permute-start.6 = (bf16[30,3,704]{2,1,0:T(4,128)(2,1)S(1)}, bf16[30,3,704]{2,1,0:T(4,128)(2,1)S(1)}, u32[]{:S(2)}, u32[]{:S(2)}) collective-permute-start(bf16[30,3,704]{2,1,0:T(4,128)(2,1)S(1)} %get-tuple-element.67), channel_id=1, source_target_pairs={{2,0},{4,2},{6,4},{3,1},{5,3},{7,5},{10,8},{12,10},{14,12},{11,9},... | collective-permute-start | bytes 380168 | tf_op jit(solution)/shard_map/ppermute | solution.py:20
  308.5 4.1 %collective-permute-start.7 = (bf16[30,3,704]{2,1,0:T(4,128)(2,1)S(1)}, bf16[30,3,704]{2,1,0:T(4,128)(2,1)S(1)}, u32[]{:S(2)}, u32[]{:S(2)}) collective-permute-start(bf16[30,3,704]{2,1,0:T(4,128)(2,1)S(1)} %get-tuple-element.68), channel_id=1, source_target_pairs={{0,2},{2,4},{4,6},{1,3},{3,5},{5,7},{8,10},{10,12},{12,14},{9,11},... | collective-permute-start | bytes 380168 | tf_op jit(solution)/shard_map/ppermute | solution.py:17
  313.1 15.8 %copy-start.4 = (f32[704]{0:T(1024)S(1)}, f32[704]{0:T(1024)}, u32[]{:S(2)}) copy-start(f32[704]{0:T(1024)} %param.23) | copy-start | bytes 8452
Sparse Core Ops, SparseCore 0:
  41.2 25.5 all-gather.3
  68.9 21.6 all-gather.7
  92.8 71.9 all-gather.5
  229.2 64.8 all-reduce.2
  296.3 32.5 reduce-scatter.1
where the time goes:
time: 339 us; the launch traced here: 338 us
  waiting for transfers between devices  180 us (53%)
  matrix products  40.4 us (12%)
  blocking collectives  39.6 us (12%)
  other arithmetic  33.2 us (10%)
  starting transfers between devices  18.3 us (5%)
  between operations  15.4 us (5%)
  local copies, waits for them, and re-layouts  11 us (3%)
    all_gather x1, waiting for transfers between devices, shards(): down_whole = lax.all_gather(down_weight, ('sy', 'sx'), axis=1, tiled=True)  74.2 us
    psum x1, waiting for transfers between devices, shards(): normed_grad = lax.psum(grad_terms, 'tp')  54.7 us
    psum x1, blocking collectives, global_vector(): return lax.psum(placed, ('sy', 'sx', 'tp'))  39.6 us
    all_gather x2, waiting for transfers between devices, all_channels(): return lax.all_gather(rows_array, 'tp', axis=1, tiled=True)  36 us
    convert_element_type x1, other arithmetic, shards(): convolved = (depthwise(extend(features), depth_kernel, image_rows, image_...  14.1 us
    ppermute x4, starting transfers between devices, extended(): lax.ppermute(lax.slice_in_dim(block, block.shape[dim] - width, None, axis...  12.9 us
    dot_general x1, matrix products, shards(): lax.dot_general(preact_grad, up_weight, contract_last, preferred_element_...  12.4 us
    convert_element_type x1, other arithmetic, shards(): feature_grad = (cotangent.astype(jnp.float32) + depthwise(extend(grad_ima...  10.3 us
  transfers between devices with their start and end apart: 13, of which 10 were waited for; matrix products, arithmetic and copies ran while one was open for 12% of the time, Pallas kernels for 0%

commit v1 on v0

--- a/solution.py
+++ b/solution.py
@@ -7,6 +7,12 @@
 TILE = 8
 root_half = 0.7071067811865476
 root_two_pi_inv = 0.3989422804014327
+
+
+def summed_here(x, axis):
+    blocks = lax.all_gather(x, axis, axis=0, tiled=False)
+    total = blocks.sum(axis=0)
+    return total
 
 
 def extended(block, sides, width):
@@ -137,7 +143,7 @@
     grad_terms = lax.dot_general(
         preact_grad, up_weight, contract_last, preferred_element_type=jnp.float32
     )
-    normed_grad = lax.psum(grad_terms, "tp")
+    normed_grad = summed_here(grad_terms, "tp")
     scaled = normed_grad * norm_gain
     convolved_grad = inv_scale * (
         scaled

time: 339 us -> 355 us (1.047)
  waiting for transfers between devices: 180 us -> 187 us
  other arithmetic: 33.2 us -> 38.1 us
    psum x1 -> x0, waiting for transfers between devices: 54.7 us -> none  [shards(): normed_grad = lax.psum(grad_terms, 'tp')]
    all_gather x0 -> x1, waiting for transfers between devices: none -> 48.4 us  [summed_here(): blocks = lax.all_gather(x, axis, axis=0, tiled=False)]
    reduce_scatter x1, waiting for transfers between devices: 5.44 us -> 24.9 us  [shards(): lax.psum_scatter(partial_out, 'tp', scatter_dimension=1, tiled=True)]
    ppermute x4, waiting for transfers between devices: 7.82 us -> 2.59 us  [extended(): lax.ppermute(lax.slice_in_dim(block, 0, width, axis=dim), axis, backward)]
  transfers between devices with their start and end apart: 13 -> 13, of which waited for: 10 -> 7; matrix products, arithmetic and copies ran while one was open for 12% -> 10% of each run, Pallas kernels for 0% -> 0%
where the time goes in v1:
time: 355 us; the launch traced here: 353 us
  waiting for transfers between devices  187 us (53%)
  matrix products  40.5 us (11%)
  blocking collectives  39.6 us (11%)
  other arithmetic  38.1 us (11%)
  starting transfers between devices  18.2 us (5%)
  between operations  16.7 us (5%)
  local copies, waits for them, and re-layouts  12.6 us (4%)
    all_gather x1, waiting for transfers between devices, shards(): down_whole = lax.all_gather(down_weight, ('sy', 'sx'), axis=1, tiled=True)  74.2 us
    all_gather x1, waiting for transfers between devices, summed_here(): blocks = lax.all_gather(x, axis, axis=0, tiled=False)  48.4 us
    psum x1, blocking collectives, global_vector(): return lax.psum(placed, ('sy', 'sx', 'tp'))  39.6 us
    all_gather x2, waiting for transfers between devices, all_channels(): return lax.all_gather(rows_array, 'tp', axis=1, tiled=True)  36.3 us
    reduce_scatter x1, waiting for transfers between devices, shards(): lax.psum_scatter(partial_out, 'tp', scatter_dimension=1, tiled=True)  24.9 us
    convert_element_type x1, other arithmetic, shards(): convolved = (depthwise(extend(features), depth_kernel, image_rows, image_...  15.1 us
    ppermute x4, starting transfers between devices, extended(): lax.ppermute(lax.slice_in_dim(block, block.shape[dim] - width, None, axis...  12.9 us
    dot_general x1, matrix products, shards(): lax.dot_general(preact_grad, up_weight, contract_last, preferred_element_...  12.4 us
  transfers between devices with their start and end apart: 13, of which 7 were waited for; matrix products, arithmetic and copies ran while one was open for 10% of the time, Pallas kernels for 0%

profile of v1, /device:TPU:0, one launch (start us, length us, event | category | flops | bytes accessed | tf_op | source)
XLA Modules:
  0.0 352.8 jit_solution(1323382839951348621)
XLA Ops:
  7.2 0.0 all-gather.6.cloned.1.call-start
  7.2 0.9 fusion.105
  8.1 4.9 %collective-permute-start = (bf16[3,16,704]{2,1,0:T(8,128)(2,1)S(1)}, bf16[3,16,704]{2,1,0:T(8,128)(2,1)S(1)}, u32[]{:S(2)}, u32[]{:S(2)}) collective-permute-start(bf16[3,16,704]{2,1,0:T(8,128)(2,1)S(1)} %get-tuple-element.77), channel_id=1, source_target_pairs={{0,8},{8,16},{16,24},{1,9},{9,17},{17,25},{2,10},{10,18},{18,26},{... | collective-permute-start | bytes 202760 | tf_op jit(solution)/shard_map/ppermute | solution.py:23
  13.1 1.3 collective-permute-start.1
  14.4 1.4 slice_reduce_fusion.48
  15.9 1.1 slice_reduce_fusion.46
  17.2 1.2 constant_dynamic-update-slice_fusion.3
  18.4 0.9 collective-permute-done.1
  19.3 0.1 fusion.103
  19.5 1.3 collective-permute-start.2
  20.8 1.3 collective-permute-start.3
  22.1 2.0 slice_reduce_fusion.47
  24.2 1.6 collective-permute-done.3
  26.1 15.1 %add_convert_fusion.2 = bf16[24,16,704]{2,1,0:T(8,128)(2,1)S(1)} fusion(bf16[24,16,704]{2,1,0:T(8,128)(2,1)S(1)} %copy-done, bf16[30,16,704]{2,1,0:T(8,128)(2,1)S(1)} %get-tuple-element.81, bf16[30,3,704]{2,1,0:T(4,128)(2,1)S(1)} %collective-permute-done.3, bf16[30,3,704]{2,1,0:T(4,128)(2,1)S(1)} %collective-permute-done.2, ...), kind=kLoop, calls=%fused_computation.149 | loop fusion | flops 74072064 | bytes 5395456 | tf_op jit(solution)/shard_map/convert_element_type | solution.py:102
  41.4 1.0 copy.29
  42.4 0.0 all-gather.6.cloned.1.call-update
  42.4 0.0 all-gather.10.cloned.1.call-start
  42.5 0.1 broadcast_in_dim.4
  42.6 0.1 convert_element_type.364
  42.6 0.1 copy.34
  42.7 0.1 broadcast_in_dim.5.clone
  42.8 0.1 convert_element_type.419
  42.9 0.2 copy.33
  43.2 0.9 multiply_convert_fusion.1
  44.0 0.0 all-gather.10.cloned.1.call-update
  44.1 0.0 all-gather.8.cloned.1.call-start
  44.1 0.7 all-gather.8.cloned.1.call-update
  44.8 0.0 all-gather.12.cloned.1.call-start
  44.9 23.5 %all-gather.6.cloned.1.call-done = bf16[384,1408]{0,1:T(8,128)(2,1)} async-done(((bf16[384,704]{0,1:T(8,128)(2,1)}), bf16[384,1408]{0,1:T(8,128)(2,1)}) %all-gather.6.cloned.1.call-update) | async-done | bytes 1081360 | tf_op jit(solution)/shard_map/all_gather | solution.py:59
  68.4 1.7 copy.30
  70.1 0.2 convert_reduce_fusion
  70.3 0.4 fusion.15
  70.8 0.0 copy-done.87
  70.8 8.6 %convolution_add_fusion = f32[384,2816]{1,0:T(8,128)} fusion(bf16[1408,2816]{1,0:T(8,128)(2,1)} %param.18, f32[2816]{0:T(1024)S(1)} %copy-done.87, f32[1408]{0:T(1024)S(1)} %copy-done.89, f32[1408]{0:T(1024)S(1)} %copy-done.83, bf16[384,1408]{1,0:T(8,128)(2,1)S(1)} %copy.30, f32[384]{0:T(512)S(1)} %add_rsqrt_fusion, f32[384]{0:T(512)S(1)} %broadcast_multiply_fusion.3), kind=kOutput, calls=%fused_computation.62 | convolution fusion | flops 3049390080 | bytes 13362176 | tf_op jit(solution)/shard_map/dot_general | solution.py:109
  79.4 12.8 %all-gather.10.cloned.1.call-done = bf16[384,1408]{0,1:T(8,128)(2,1)} async-done(((bf16[384,704]{0,1:T(8,128)(2,1)}), bf16[384,1408]{0,1:T(8,128)(2,1)}) %all-gather.10.cloned.1.call-update) | async-done | bytes 1081360 | tf_op jit(solution)/shard_map/all_gather | solution.py:59
  92.2 74.2 %all-gather.8.cloned.1.call-done = bf16[2816,1408]{0,1:T(8,128)(2,1)} async-done(((bf16[2816,88]{0,1:T(8,128)(2,1)}), bf16[2816,1408]{0,1:T(8,128)(2,1)}) %all-gather.8.cloned.1.call-update) | async-done | bytes 7929872 | tf_op jit(solution)/shard_map/all_gather | solution.py:121
  166.4 9.9 %fusion.10 = (f32[2816]{0:T(1024)S(1)}, f32[2816]{0:T(1024)S(1)}, bf16[384,2816]{1,0:T(8,128)(2,1)}, f32[384,2816]{1,0:T(8,128)}) fusion(f32[384]{0:T(512)S(1)} %convert_element_type.419, f32[384,2816]{1,0:T(8,128)} %convolution_add_fusion, bf16[384,1408]{0,1:T(8,128)(2,1)} %all-gather.10.cloned.1.call-done, bf16[2816,1408]{0,1:T(8,128)(2,1)} %all-gather.8.cloned.1.call-done), kind=kOutput, calls=%fused_computation.57 | convolution fusion | flops 3056953856 | bytes 19848704 | tf_op jit(solution)/shard_map/dot_general | solution.py:130
  176.3 0.3 dynamic_update_slice.6
  176.6 0.1 multiply_dynamic-update-slice_fusion
  176.8 39.6 %all-reduce = (f32[5632]{0:T(1024)S(1)}, f32[5632]{0:T(1024)S(1)}) all-reduce(f32[5632]{0:T(1024)S(1)} %dynamic_update_slice.6, f32[5632]{0:T(1024)S(1)} %multiply_dynamic-update-slice_fusion), channel_id=1, replica_groups=mesh['sy'=4,'sx'=4,'tp'=2] {'sy','sx','tp'}, use_global_device_ids=true, to_apply=%region_3.0 | all-reduce | flops 11264 | bytes 90112 | tf_op jit(solution)/shard_map/psum | solution.py:69
  216.3 0.6 multiply_reduce_fusion.1
  218.2 0.1 multiply_add_fusion
  218.3 12.4 %fusion.21 = f32[384,1408]{1,0:T(8,128)} fusion(bf16[1408,2816]{1,0:T(8,128)(2,1)} %param.18, f32[384,2816]{1,0:T(8,128)} %convolution_add_fusion, bf16[384,2816]{1,0:T(8,128)(2,1)} %get-tuple-element.63, f32[384,2816]{1,0:T(8,128)} %get-tuple-element.83, f32[2816]{0:T(1024)S(1)} %get-tuple-element.62, f32[2816]{0:T(1024)S(1)} %get-tuple-element.84, ...), kind=kOutput, calls=%fused_computation.74 | convolution fusion | flops 3062366208 | bytes 20941312 | tf_op jit(solution)/shard_map/dot_general | solution.py:143
  230.7 0.0 all-gather.12.cloned.1.call-update
  230.7 0.0 reduce-scatter.2.cloned.1.call-start
  230.8 0.6 copy-done.88
  231.4 9.6 %fusion.16 = f32[384,1408]{0,1:T(8,128)} fusion(bf16[2816,1408]{0,1:T(8,128)(2,1)} %all-gather.8.cloned.1.call-done, bf16[384,2816]{1,0:T(8,128)(2,1)} %get-tuple-element.63, f32[2816]{0:T(1024)S(1)} %copy-done.88, f32[2816]{0:T(1024)S(1)} %get-tuple-element.61, f32[2816]{0:T(1024)S(1)} %copy-done.4), kind=kOutput, calls=%fused_computation.68 | convolution fusion | flops 3051552768 | bytes 12289024 | tf_op jit(solution)/shard_map/dot_general | solution.py:122
  241.1 0.1 copy.28
  241.2 48.4 %all-gather.12.cloned.1.call-done = f32[768,1408]{1,0:T(8,128)} async-done(((f32[384,1408]{1,0:T(8,128)}), f32[768,1408]{1,0:T(8,128)}) %all-gather.12.cloned.1.call-update) | async-done | bytes 4325392 | tf_op jit(solution)/shard_map/all_gather | solution.py:13
  289.6 2.7 reduce_sum.87
  292.3 0.7 fusion.102
  293.1 1.0 fusion.51
  294.0 0.7 fusion.104
  294.7 3.4 collective-permute-start.4
  298.1 1.3 collective-permute-start.5
  299.4 24.9 %reduce-scatter.2.cloned.1.call-done = f32[384,704]{0,1:T(8,128)} async-done(((f32[384,1408]{0,1:T(8,128)}), f32[384,704]{0,1:T(8,128)}) %reduce-scatter.2.cloned.1.call-update) | async-done | bytes 1081360 | tf_op jit(solution)/shard_map/reduce_scatter | solution.py:123
  324.3 1.4 broadcast_add_fusion
  325.7 0.4 copy.32
  326.1 0.9 pad_maximum_fusion.7
  327.1 1.3 collective-permute-start.6
  328.4 3.3 collective-permute-start.7
  331.6 1.0 fusion.48
  333.1 1.5 pad_maximum_fusion
  335.0 11.3 %add_convert_fusion.1 = bf16[24,16,704]{2,1,0:T(8,128)(2,1)} fusion(bf16[24,16,704]{2,1,0:T(8,128)(2,1)S(1)} %bitcast.19, bf16[3,16,704]{2,1,0:T(8,128)(2,1)S(1)} %collective-permute-done.4, bf16[3,16,704]{2,1,0:T(8,128)(2,1)} %collective-permute-done.5, bf16[30,19,704]{2,1,0:T(8,128)(2,1)S(1)} %get-tuple-element.66, ...), kind=kLoop, calls=%fused_computation.148 | loop fusion | flops 41902080 | bytes 24603392 | tf_op jit(solution)/shard_map/convert_element_type | solution.py:159
  (195 shorter events, 0.5 us)
Async XLA Ops:
  7.2 61.2 %all-gather.6.cloned.1.call-start = ((), (), s32[]{:S(2)}) async-start(), calls=%async_computation.1 | async-start | bytes 1622016 | tf_op jit(solution)/shard_map/all_gather | solution.py:59
  8.1 9.0 %collective-permute-start = (bf16[3,16,704]{2,1,0:T(8,128)(2,1)S(1)}, bf16[3,16,704]{2,1,0:T(8,128)(2,1)S(1)}, u32[]{:S(2)}, u32[]{:S(2)}) collective-permute-start(bf16[3,16,704]{2,1,0:T(8,128)(2,1)S(1)} %get-tuple-element.77), channel_id=1, source_target_pairs={{0,8},{8,16},{16,24},{1,9},{9,17},{17,25},{2,10},{10,18},{18,26},{... | collective-permute-start | bytes 202760 | tf_op jit(solution)/shard_map/ppermute | solution.py:23
  13.1 6.2 %collective-permute-start.1 = (bf16[3,16,704]{2,1,0:T(8,128)(2,1)S(1)}, bf16[3,16,704]{2,1,0:T(8,128)(2,1)S(1)}, u32[]{:S(2)}, u32[]{:S(2)}) collective-permute-start(bf16[3,16,704]{2,1,0:T(8,128)(2,1)S(1)} %get-tuple-element.76), channel_id=1, source_target_pairs={{8,0},{16,8},{24,16},{9,1},{17,9},{25,17},{10,2},{18,10},{26,18},{... | collective-permute-start | bytes 202760 | tf_op jit(solution)/shard_map/ppermute | solution.py:26
  15.8 10.1 %copy-start.5 = (f32[704]{0:T(1024)}, f32[704]{0:T(1024)S(1)}, u32[]{:S(2)}) copy-start(f32[704]{0:T(1024)S(1)} %get-tuple-element.13) | copy-start | bytes 8452
  15.8 10.1 %copy-start.7 = (f32[704]{0:T(1024)}, f32[704]{0:T(1024)S(1)}, u32[]{:S(2)}) copy-start(f32[704]{0:T(1024)S(1)} %get-tuple-element.14) | copy-start | bytes 8452
  15.8 10.1 %copy-start.9 = (f32[704]{0:T(1024)}, f32[704]{0:T(1024)S(1)}, u32[]{:S(2)}) copy-start(f32[704]{0:T(1024)S(1)} %get-tuple-element.15) | copy-start | bytes 8452
  15.8 10.1 %copy-start.11 = (f32[704]{0:T(1024)}, f32[704]{0:T(1024)S(1)}, u32[]{:S(2)}) copy-start(f32[704]{0:T(1024)S(1)} %get-tuple-element.16) | copy-start | bytes 8452
  15.8 10.1 %copy-start.13 = (f32[704]{0:T(1024)}, f32[704]{0:T(1024)S(1)}, u32[]{:S(2)}) copy-start(f32[704]{0:T(1024)S(1)} %get-tuple-element.17) | copy-start | bytes 8452
  15.8 10.1 %copy-start.15 = (f32[704]{0:T(1024)}, f32[704]{0:T(1024)S(1)}, u32[]{:S(2)}) copy-start(f32[704]{0:T(1024)S(1)} %get-tuple-element.18) | copy-start | bytes 8452
  15.8 10.1 %copy-start.17 = (f32[704]{0:T(1024)}, f32[704]{0:T(1024)S(1)}, u32[]{:S(2)}) copy-start(f32[704]{0:T(1024)S(1)} %get-tuple-element.19) | copy-start | bytes 8452
  15.8 10.1 %copy-start.19 = (f32[704]{0:T(1024)}, f32[704]{0:T(1024)S(1)}, u32[]{:S(2)}) copy-start(f32[704]{0:T(1024)S(1)} %get-tuple-element.20) | copy-start | bytes 8452
  15.8 10.1 %copy-start.21 = (f32[704]{0:T(1024)}, f32[704]{0:T(1024)S(1)}, u32[]{:S(2)}) copy-start(f32[704]{0:T(1024)S(1)} %get-tuple-element.21) | copy-start | bytes 8452
  15.9 10.1 %copy-start.23 = (f32[704]{0:T(1024)}, f32[704]{0:T(1024)S(1)}, u32[]{:S(2)}) copy-start(f32[704]{0:T(1024)S(1)} %get-tuple-element.22) | copy-start | bytes 8452
  15.9 10.1 %copy-start.25 = (f32[704]{0:T(1024)}, f32[704]{0:T(1024)S(1)}, u32[]{:S(2)}) copy-start(f32[704]{0:T(1024)S(1)} %get-tuple-element.23) | copy-start | bytes 8452
  15.9 10.1 %copy-start.27 = (f32[704]{0:T(1024)}, f32[704]{0:T(1024)S(1)}, u32[]{:S(2)}) copy-start(f32[704]{0:T(1024)S(1)} %get-tuple-element.24) | copy-start | bytes 8452
  17.0 9.0 %copy-start.29 = (f32[704]{0:T(1024)}, f32[704]{0:T(1024)S(1)}, u32[]{:S(2)}) copy-start(f32[704]{0:T(1024)S(1)} %get-tuple-element.44) | copy-start | bytes 8452
  17.0 9.0 %copy-start.31 = (f32[704]{0:T(1024)}, f32[704]{0:T(1024)S(1)}, u32[]{:S(2)}) copy-start(f32[704]{0:T(1024)S(1)} %get-tuple-element.45) | copy-start | bytes 8452
  17.0 9.0 %copy-start.33 = (f32[704]{0:T(1024)}, f32[704]{0:T(1024)S(1)}, u32[]{:S(2)}) copy-start(f32[704]{0:T(1024)S(1)} %get-tuple-element.46) | copy-start | bytes 8452
  17.1 9.0 %copy-start.35 = (f32[704]{0:T(1024)}, f32[704]{0:T(1024)S(1)}, u32[]{:S(2)}) copy-start(f32[704]{0:T(1024)S(1)} %get-tuple-element.47) | copy-start | bytes 8452
  17.1 9.0 %copy-start.37 = (f32[704]{0:T(1024)}, f32[704]{0:T(1024)S(1)}, u32[]{:S(2)}) copy-start(f32[704]{0:T(1024)S(1)} %get-tuple-element.48) | copy-start | bytes 8452
  17.1 9.0 %copy-start.39 = (f32[704]{0:T(1024)}, f32[704]{0:T(1024)S(1)}, u32[]{:S(2)}) copy-start(f32[704]{0:T(1024)S(1)} %get-tuple-element.49) | copy-start | bytes 8452
  17.1 9.0 %copy-start.41 = (f32[704]{0:T(1024)}, f32[704]{0:T(1024)S(1)}, u32[]{:S(2)}) copy-start(f32[704]{0:T(1024)S(1)} %get-tuple-element.50) | copy-start | bytes 8452
  17.1 9.0 %copy-start.43 = (f32[704]{0:T(1024)}, f32[704]{0:T(1024)S(1)}, u32[]{:S(2)}) copy-start(f32[704]{0:T(1024)S(1)} %get-tuple-element.51) | copy-start | bytes 8452
  17.1 9.0 %copy-start.45 = (f32[704]{0:T(1024)}, f32[704]{0:T(1024)S(1)}, u32[]{:S(2)}) copy-start(f32[704]{0:T(1024)S(1)} %get-tuple-element.52) | copy-start | bytes 8452
  17.1 9.0 %copy-start.47 = (f32[704]{0:T(1024)}, f32[704]{0:T(1024)S(1)}, u32[]{:S(2)}) copy-start(f32[704]{0:T(1024)S(1)} %get-tuple-element.53) | copy-start | bytes 8452
  17.1 9.0 %copy-start.49 = (f32[704]{0:T(1024)}, f32[704]{0:T(1024)S(1)}, u32[]{:S(2)}) copy-start(f32[704]{0:T(1024)S(1)} %get-tuple-element.54) | copy-start | bytes 8452
  18.4 7.7 %copy-start = (bf16[24,16,704]{2,1,0:T(8,128)(2,1)S(1)}, bf16[24,16,704]{2,1,0:T(8,128)(2,1)}, u32[]{:S(2)}) copy-start(bf16[24,16,704]{2,1,0:T(8,128)(2,1)} %param.13) | copy-start | bytes 1622020
  18.4 7.7 %copy-start.85 = (f32[704]{0:T(1024)S(1)}, f32[704]{0:T(1024)}, u32[]{:S(2)}) copy-start(f32[704]{0:T(1024)} %param.15) | copy-start | bytes 8452
  19.5 4.7 %collective-permute-start.2 = (bf16[30,3,704]{2,1,0:T(4,128)(2,1)S(1)}, bf16[30,3,704]{2,1,0:T(4,128)(2,1)S(1)}, u32[]{:S(2)}, u32[]{:S(2)}) collective-permute-start(bf16[30,3,704]{2,1,0:T(4,128)(2,1)S(1)} %get-tuple-element.69), channel_id=1, source_target_pairs={{0,2},{2,4},{4,6},{1,3},{3,5},{5,7},{8,10},{10,12},{12,14},{9,11},... | collective-permute-start | bytes 380168 | tf_op jit(solution)/shard_map/ppermute | solution.py:23
  20.8 5.1 %collective-permute-start.3 = (bf16[30,3,704]{2,1,0:T(4,128)(2,1)S(1)}, bf16[30,3,704]{2,1,0:T(4,128)(2,1)S(1)}, u32[]{:S(2)}, u32[]{:S(2)}) collective-permute-start(bf16[30,3,704]{2,1,0:T(4,128)(2,1)S(1)} %get-tuple-element.70), channel_id=1, source_target_pairs={{2,0},{4,2},{6,4},{3,1},{5,3},{7,5},{10,8},{12,10},{14,12},{11,9},... | collective-permute-start | bytes 380168 | tf_op jit(solution)/shard_map/ppermute | solution.py:26
  24.1 17.1 %copy-start.51 = (f32[704]{0:T(1024)}, f32[704]{0:T(1024)S(1)}, u32[]{:S(2)}) copy-start(f32[704]{0:T(1024)S(1)} %get-tuple-element.25) | copy-start | bytes 8452
  24.1 17.1 %copy-start.53 = (f32[704]{0:T(1024)}, f32[704]{0:T(1024)S(1)}, u32[]{:S(2)}) copy-start(f32[704]{0:T(1024)S(1)} %get-tuple-element.26) | copy-start | bytes 8452
  24.1 17.1 %copy-start.55 = (f32[704]{0:T(1024)}, f32[704]{0:T(1024)S(1)}, u32[]{:S(2)}) copy-start(f32[704]{0:T(1024)S(1)} %get-tuple-element.27) | copy-start | bytes 8452
  24.1 17.1 %copy-start.57 = (f32[704]{0:T(1024)}, f32[704]{0:T(1024)S(1)}, u32[]{:S(2)}) copy-start(f32[704]{0:T(1024)S(1)} %get-tuple-element.28) | copy-start | bytes 8452
  24.1 17.1 %copy-start.59 = (f32[704]{0:T(1024)}, f32[704]{0:T(1024)S(1)}, u32[]{:S(2)}) copy-start(f32[704]{0:T(1024)S(1)} %get-tuple-element.29) | copy-start | bytes 8452
  24.1 17.1 %copy-start.61 = (f32[704]{0:T(1024)}, f32[704]{0:T(1024)S(1)}, u32[]{:S(2)}) copy-start(f32[704]{0:T(1024)S(1)} %get-tuple-element.30) | copy-start | bytes 8452
  24.1 17.1 %copy-start.63 = (f32[704]{0:T(1024)}, f32[704]{0:T(1024)S(1)}, u32[]{:S(2)}) copy-start(f32[704]{0:T(1024)S(1)} %get-tuple-element.31) | copy-start | bytes 8452
  24.1 17.1 %copy-start.65 = (f32[704]{0:T(1024)}, f32[704]{0:T(1024)S(1)}, u32[]{:S(2)}) copy-start(f32[704]{0:T(1024)S(1)} %get-tuple-element.32) | copy-start | bytes 8452
  24.1 17.1 %copy-start.67 = (f32[704]{0:T(1024)}, f32[704]{0:T(1024)S(1)}, u32[]{:S(2)}) copy-start(f32[704]{0:T(1024)S(1)} %get-tuple-element.33) | copy-start | bytes 8452
  24.2 17.1 %copy-start.69 = (f32[704]{0:T(1024)}, f32[704]{0:T(1024)S(1)}, u32[]{:S(2)}) copy-start(f32[704]{0:T(1024)S(1)} %get-tuple-element.34) | copy-start | bytes 8452
  24.2 17.1 %copy-start.71 = (f32[704]{0:T(1024)}, f32[704]{0:T(1024)S(1)}, u32[]{:S(2)}) copy-start(f32[704]{0:T(1024)S(1)} %get-tuple-element.35) | copy-start | bytes 8452
  24.2 17.1 %copy-start.73 = (f32[704]{0:T(1024)}, f32[704]{0:T(1024)S(1)}, u32[]{:S(2)}) copy-start(f32[704]{0:T(1024)S(1)} %get-tuple-element.36) | copy-start | bytes 8452
  24.2 17.1 %copy-start.75 = (f32[704]{0:T(1024)}, f32[704]{0:T(1024)S(1)}, u32[]{:S(2)}) copy-start(f32[704]{0:T(1024)S(1)} %get-tuple-element.37) | copy-start | bytes 8452
  24.2 17.1 %copy-start.77 = (f32[704]{0:T(1024)}, f32[704]{0:T(1024)S(1)}, u32[]{:S(2)}) copy-start(f32[704]{0:T(1024)S(1)} %get-tuple-element.38) | copy-start | bytes 8452
  24.2 17.1 %copy-start.79 = (f32[704]{0:T(1024)}, f32[704]{0:T(1024)S(1)}, u32[]{:S(2)}) copy-start(f32[704]{0:T(1024)S(1)} %get-tuple-element.39) | copy-start | bytes 8452
  24.2 17.1 %copy-start.81 = (f32[704]{0:T(1024)}, f32[704]{0:T(1024)S(1)}, u32[]{:S(2)}) copy-start(f32[704]{0:T(1024)S(1)} %get-tuple-element.40) | copy-start | bytes 8452
  42.4 49.8 %all-gather.10.cloned.1.call-start = ((), (), s32[]{:S(2)}) async-start(), calls=%async_computation.4 | async-start | bytes 1622016 | tf_op jit(solution)/shard_map/all_gather | solution.py:59
  44.1 122.3 %all-gather.8.cloned.1.call-start = ((), (), s32[]{:S(2)}) async-start(), calls=%async_computation.2 | async-start | bytes 8425472 | tf_op jit(solution)/shard_map/all_gather | solution.py:121
  44.8 244.8 %all-gather.12.cloned.1.call-start = ((), (), s32[]{:S(2)}) async-start(), calls=%async_computation.5 | async-start | bytes 6488064 | tf_op jit(solution)/shard_map/all_gather | solution.py:13
  79.4 97.2 %copy-start.4 = (f32[2816]{0:T(1024)S(1)}, f32[2816]{0:T(1024)}, u32[]{:S(2)}) copy-start(f32[2816]{0:T(1024)} %param.20) | copy-start | bytes 33796
  230.7 93.6 %reduce-scatter.2.cloned.1.call-start = ((), (), s32[]{:S(2)}) async-start(), calls=%async_computation.3 | async-start | bytes 3244032 | tf_op jit(solution)/shard_map/reduce_scatter | solution.py:123
  293.0 31.3 %copy-start.84 = (f32[704]{0:T(1024)S(1)}, f32[704]{0:T(1024)}, u32[]{:S(2)}) copy-start(f32[704]{0:T(1024)} %param.23) | copy-start | bytes 8452
  294.7 31.4 %collective-permute-start.4 = (bf16[3,16,704]{2,1,0:T(8,128)(2,1)}, bf16[3,16,704]{2,1,0:T(8,128)(2,1)S(1)}, u32[]{:S(2)}, u32[]{:S(2)}) collective-permute-start(bf16[3,16,704]{2,1,0:T(8,128)(2,1)} %bitcast.5), channel_id=1, source_target_pairs={{0,8},{8,16},{16,24},{1,9},{9,17},{17,25},{2,10},{10,18},{18,26},{... | collective-permute-start | bytes 202760 | tf_op jit(solution)/shard_map/ppermute | solution.py:23
  298.1 28.0 %collective-permute-start.5 = (bf16[3,16,704]{2,1,0:T(8,128)(2,1)}, bf16[3,16,704]{2,1,0:T(8,128)(2,1)}, u32[]{:S(2)}, u32[]{:S(2)}) collective-permute-start(bf16[3,16,704]{2,1,0:T(8,128)(2,1)} %bitcast.7), channel_id=1, source_target_pairs={{8,0},{16,8},{24,16},{9,1},{17,9},{25,17},{10,2},{18,10},{26,18},{... | collective-permute-start | bytes 202760 | tf_op jit(solution)/shard_map/ppermute | solution.py:26
  325.7 5.9 %copy-start.1 = (bf16[24,16,704]{2,1,0:T(8,128)(2,1)S(1)}, bf16[24,16,704]{2,1,0:T(8,128)(2,1)}, u32[]{:S(2)}) copy-start(bf16[24,16,704]{2,1,0:T(8,128)(2,1)} %param.13) | copy-start | bytes 1622020
  327.1 6.0 %collective-permute-start.6 = (bf16[30,3,704]{2,1,0:T(4,128)(2,1)S(1)}, bf16[30,3,704]{2,1,0:T(4,128)(2,1)S(1)}, u32[]{:S(2)}, u32[]{:S(2)}) collective-permute-start(bf16[30,3,704]{2,1,0:T(4,128)(2,1)S(1)} %get-tuple-element.67), channel_id=1, source_target_pairs={{2,0},{4,2},{6,4},{3,1},{5,3},{7,5},{10,8},{12,10},{14,12},{11,9},... | collective-permute-start | bytes 380168 | tf_op jit(solution)/shard_map/ppermute | solution.py:26
  328.4 4.7 %collective-permute-start.7 = (bf16[30,3,704]{2,1,0:T(4,128)(2,1)S(1)}, bf16[30,3,704]{2,1,0:T(4,128)(2,1)S(1)}, u32[]{:S(2)}, u32[]{:S(2)}) collective-permute-start(bf16[30,3,704]{2,1,0:T(4,128)(2,1)S(1)} %get-tuple-element.68), channel_id=1, source_target_pairs={{0,2},{2,4},{4,6},{1,3},{3,5},{5,7},{8,10},{10,12},{12,14},{9,11},... | collective-permute-start | bytes 380168 | tf_op jit(solution)/shard_map/ppermute | solution.py:23
  332.7 1.9 copy-start.12
  332.7 1.9 copy-start.14
  332.7 1.9 copy-start.16
  332.7 1.9 copy-start.18
  332.7 1.9 copy-start.20
  332.7 1.9 copy-start.22
  332.7 1.9 copy-start.24
  (39 other events, 69.5 us)
Sparse Core Ops, SparseCore 0:
  42.5 25.7 all-gather.5
  70.5 21.6 all-gather.9
  94.4 71.9 all-gather.7
  230.9 58.6 all-gather.11
  291.7 32.5 reduce-scatter.1
